TPU v7x, 32 devices: a whole 2x2x4 slice. The times are simulated.
32 devices in a mesh: section: 2 (over y), ident: 16 (over z, x, core).
Axes of the slice: x: 2, y: 2, z: 4, core: 2. Of those that a mesh axis runs over, the one named last changes fastest.
Arguments:
- inputs: bfloat16 [16, 192, 1024], P('ident'), may hold values from -6 to 6
- section_weight: bfloat16 [2, 1024, 1024], P('section'), may hold values from -0.1875 to 0.1875
- section_gain: float32 [2, 1024], P('section'), may hold values from 0.25 to 1.75
- neck_weight: bfloat16 [1024, 512], replicated, may hold values from -0.1875 to 0.1875
- centers: bfloat16 [16, 2, 3, 128, 512], P('ident'), may hold values from -6 to 6
- sampled: int32 [16, 2], P('ident'), may hold values from 0 to 255, as said below
- labels: int32 [16, 192], P('ident', 'section'), may hold values from 0 to 524287, as said below
Outputs:
- embed_grad: float32 [16, 192, 512], P('ident', 'section')
Inputs may be any that keep to these rules, and one draw needn't show every extreme that they name: `sampled`: the 2 block numbers of one shard are distinct. `labels`: every label is i * 256 * 128 + sampled[i, a] 128 + t for some shard i, slot a and position t.
All inputs are finite; a program needn't handle non-finite values.
Results may differ from a plain program's by a relative error of at most 0.008.
Values may be sent and summed in bfloat16 or wider, within the bound.
A program may use at most 64 MiB of HBM per device.

v0:
```python
import math

import jax
import jax.numpy as jnp
from jax import lax
from jax.sharding import PartitionSpec as P

BLOCKS_DEV = 256


logit_scale = 64.0
pool_temp = 0.1
margin_angle = 0.5
sine_offset = 1.05


def from_behind(block, axis, distance):
    devices = range(lax.axis_size(axis))
    route = [(i - distance, i) for i in devices if i - distance in devices]
    return lax.ppermute(block, axis, route)


def broadcast(block, axis, owner):
    block = jnp.where(lax.axis_index(axis) == owner, block, jnp.zeros_like(block))
    return lax.psum(block, axis)


def layer_norm(values, gain):
    valf = values.astype(jnp.float32)
    center = valf - jnp.mean(valf, axis=-1, keepdims=True)
    spread = jnp.mean(center * center, axis=-1, keepdims=True)
    return center * lax.rsqrt(spread + 1e-06) * gain


def section_apply(trunk, weight, gain):
    normed = layer_norm(trunk, gain).astype(jnp.bfloat16)
    mixed = jnp.dot(normed, weight, preferred_element_type=jnp.float32)
    return (trunk.astype(jnp.float32) + jax.nn.gelu(mixed, approximate=False)).astype(jnp.bfloat16)


def neck_apply(trunk, neck_weight):
    neck_in = layer_norm(trunk, 1.0).astype(jnp.bfloat16)
    return jnp.dot(neck_in, neck_weight, preferred_element_type=jnp.float32).astype(jnp.bfloat16)


def unit_rows(values):
    valf = values.astype(jnp.float32)
    inverse = lax.rsqrt(jnp.sum(valf * valf, axis=-1, keepdims=True) + 1e-06)
    return (valf * inverse, inverse)


def shards(inputs, section_weight, section_gain, neck_weight, centers, sampled, labels):
    sections = lax.axis_size("section")
    section_index = lax.axis_index("section")
    shard_index = lax.axis_index("ident")
    trunk = inputs[0]
    weight = section_weight[0]
    section_scale = section_gain[0]
    rows_all = trunk.shape[0]
    head_rows = rows_all // sections
    hidden = trunk
    for turn in range(sections):
        hidden = section_apply(hidden, weight, section_scale)
        if turn + 1 < sections:
            hidden = from_behind(hidden, "section", 1)
    embed_all = neck_apply(hidden, neck_weight)
    embed_all = broadcast(embed_all, "section", sections - 1)
    own_embed = lax.dynamic_slice_in_dim(embed_all, section_index * head_rows, head_rows, 0)
    direction, inverse = unit_rows(own_embed)
    unit_own = direction.astype(jnp.bfloat16)
    gathered, gathered_labels = (
        lax.all_gather(unit_own[None], "ident", axis=0, tiled=True),
        lax.all_gather(labels, "ident", axis=0, tiled=True),
    )
    width = centers.shape[-1]
    nsamp = centers.shape[1]
    nsub = centers.shape[2]
    nblk = centers.shape[3]
    feature = gathered.reshape(-1, width)
    label_flat = gathered_labels.reshape(-1)
    row_count = feature.shape[0]
    unit_centers = unit_rows(centers[0].reshape(-1, width))[0].astype(jnp.bfloat16)
    cosine = lax.dot_general(
        feature, unit_centers, (((1,), (1,)), ((), ())), preferred_element_type=jnp.float32
    )
    cosine = cosine.reshape(row_count, nsamp, nsub, nblk)
    expo = jnp.exp(cosine / pool_temp)
    summed = jnp.sum(expo, axis=2)
    pooled = pool_temp * jnp.log(summed / nsub)
    weights = expo / summed[:, :, None, :]
    idents = (
        shard_index * (BLOCKS_DEV * nblk)
        + sampled[0][:, None] * nblk
        + jnp.arange(nblk, dtype=jnp.int32)[None, :]
    )
    target = label_flat[:, None, None] == idents[None, :, :]
    root_term = jnp.sqrt(sine_offset - pooled * pooled)
    margin = pooled * math.cos(margin_angle) - root_term * math.sin(margin_angle)
    logits = logit_scale * jnp.where(target, margin, pooled)
    slope = jnp.where(
        target, math.cos(margin_angle) + pooled * math.sin(margin_angle) / root_term, 1.0
    )
    exp_logits = jnp.exp(logits)
    totals = lax.psum(jnp.sum(exp_logits, axis=(1, 2)), "ident")
    factor = logit_scale * (exp_logits / totals[:, None, None] - target.astype(jnp.float32)) * slope
    pulled = (factor[:, :, None, :] * weights).astype(jnp.bfloat16).reshape(row_count, -1)
    own_grad = lax.psum_scatter(
        jnp.dot(pulled, unit_centers, preferred_element_type=jnp.float32),
        "ident",
        scatter_dimension=0,
        tiled=True,
    )
    along = jnp.sum(own_grad * direction, axis=-1, keepdims=True)
    embed_grad = inverse * (own_grad - along * direction)
    return embed_grad[None]


def solution(mesh):
    in_specs = (
        P("ident", None, None),
        P("section", None, None),
        P("section", None),
        P(),
        P("ident", None, None, None, None),
        P("ident", None),
        P("ident", "section"),
    )
    out_specs = P("ident", "section", None)
    return jax.shard_map(shards, mesh=mesh, in_specs=in_specs, out_specs=out_specs, check_vma=False)
```

profile of v0, /device:TPU:0, one launch (start us, length us, event | category | flops | bytes accessed | tf_op | source)
XLA Modules:
  0.0 219.9 jit_solution(13767589372090451552)
XLA Ops:
  6.5 1.3 convert_reduce_fusion.1
  7.8 1.2 fusion.30
  9.1 3.4 %fusion.31 = bf16[192,1024]{1,0:T(8,128)(2,1)S(1)} fusion(bf16[1,192,1024]{2,1,0:T(8,128)(2,1)} %param.7, bf16[1,1024,1024]{2,1,0:T(8,128)(2,1)S(1)} %copy-done, f32[1024]{0:T(1024)} %bitcast.52, f32[192]{0:T(256)S(1)} %add_rsqrt_fusion.3, f32[192]{0:T(256)S(1)} %broadcast_multiply_fusion.2), kind=kOutput, calls=%fused_computation.51 | convolution fusion | flops 416808960 | bytes 2889216 | tf_op jit(solution)/shard_map/dot_general | solution.py:37
  12.5 4.9 %collective-permute-start = (bf16[192,1024]{1,0:T(8,128)(2,1)S(1)}, bf16[192,1024]{1,0:T(8,128)(2,1)S(1)}, u32[]{:S(2)}, u32[]{:S(2)}) collective-permute-start(bf16[192,1024]{1,0:T(8,128)(2,1)S(1)} %fusion.31), channel_id=1, source_target_pairs={{0,16},{1,17},{2,18},{3,19},{4,20},{5,21},{6,22},{7,23},{8,24},{9,... | collective-permute-start | bytes 1179656 | tf_op jit(solution)/shard_map/ppermute | solution.py:20
  17.4 8.3 %collective-permute-done = bf16[192,1024]{1,0:T(8,128)(2,1)S(1)} collective-permute-done((bf16[192,1024]{1,0:T(8,128)(2,1)S(1)}, bf16[192,1024]{1,0:T(8,128)(2,1)S(1)}, u32[]{:S(2)}, u32[]{:S(2)}) %collective-permute-start) | collective-permute-done | bytes 393248 | tf_op jit(solution)/shard_map/ppermute | solution.py:20
  26.2 2.4 %convert_reduce_fusion.2 = (f32[192]{0:T(256)S(1)}, bf16[192,1024]{1,0:T(8,128)(2,1)S(1)}) fusion(bf16[1,1024,1024]{2,1,0:T(8,128)(2,1)S(1)} %copy-done, bf16[192,1024]{1,0:T(8,128)(2,1)S(1)} %collective-permute-done, f32[1024]{0:T(1024)S(1)} %bitcast.53, f32[192]{0:T(256)S(1)} %add_rsqrt_fusion.2, f32[192]{0:T(256)S(1)} %broadcast_multiply_fusion.1), kind=kOutput, calls=%fused_computation.39 | convolution fusion | flops 417201984 | bytes 2889984 | tf_op jit(solution)/shard_map/dot_general | solution.py:37
  28.9 1.1 fusion.17
  30.1 24.6 %all-reduce.2.cloned.1.call-done = bf16[192,512]{1,0:T(8,128)(2,1)} async-done(((bf16[192,512]{1,0:T(8,128)(2,1)}), bf16[192,512]{1,0:T(8,128)(2,1)}) %all-reduce.2.cloned.1.call-update) | async-done | bytes 196624 | tf_op jit(solution)/shard_map/psum | solution.py:25
  54.7 1.0 fusion.78
  55.8 1.6 fusion.73
  57.5 21.2 %all-gather.1 = s32[16,1,96]{2,1,0:T(1,128)S(1)} all-gather(s32[1,1,96]{2,1,0:T(1,128)S(1)} %bitcast.51), channel_id=1, replica_groups=mesh['section'=2,'ident'=16] {'ident'}, dimensions={0}, use_global_device_ids=true | all-gather | bytes 6528 | tf_op jit(solution)/shard_map/all_gather | solution.py:73
  79.2 0.6 reduce.5
  80.2 1.1 fusion.6
  81.4 15.9 %all-gather.4.cloned.1.call-done = bf16[1536,512]{1,0:T(8,128)(2,1)} async-done(((bf16[96,512]{1,0:T(8,128)(2,1)}), bf16[1536,512]{1,0:T(8,128)(2,1)}) %all-gather.4.cloned.1.call-update) | async-done | bytes 1572880 | tf_op jit(solution)/shard_map/all_gather | solution.py:72
  97.2 5.3 %fusion = (f32[1536,2,128]{0,2,1:T(8,128)S(1)}, f32[1536,2,3,128]{0,3,2,1:T(8,128)}) fusion(bf16[1,2,3,128,512]{4,3,2,1,0:T(8,128)(2,1)} %fusion.6, bf16[1536,512]{1,0:T(8,128)(2,1)} %all-gather.4.cloned.1.call-done), kind=kOutput, calls=%fused_computation.2 | convolution fusion | flops 1209925632 | bytes 8650752 | tf_op jit(solution)/shard_map/dot_general | solution.py:83
  102.6 1.2 copy-done.1
  103.8 1.2 fusion.14
  104.9 32.3 %psum.15 = f32[1536]{0:T(1024)S(1)} all-reduce(f32[1536]{0:T(1024)S(1)} %fusion.14), channel_id=1, replica_groups=mesh['section'=2,'ident'=16] {'ident'}, use_global_device_ids=true, to_apply=%region_11.12 | all-reduce | flops 1536 | bytes 12288 | tf_op jit(solution)/shard_map/psum | solution.py:104
  137.2 3.1 %fusion.11 = f32[1536,2,128]{0,2,1:T(8,128)S(1)} fusion(f32[1536,2,128]{0,2,1:T(8,128)} %copy-done.1, f32[1536]{0:T(1024)S(1)} %psum.15, s32[2,128]{1,0:T(2,128)S(1)} %iota_add_fusion, s32[1536]{0:T(1024)S(1)} %eq.23), kind=kLoop, calls=%fused_computation.18 | loop fusion | flops 7471104 | bytes 3159040 | tf_op jit(solution)/shard_map/mul | solution.py:105
  140.4 3.5 %multiply_convert_fusion = bf16[1536,2,3,128]{0,3,2,1:T(8,128)(2,1)S(1)} fusion(f32[1536,2,3,128]{0,3,2,1:T(8,128)} %get-tuple-element.8, f32[1536,2,128]{0,2,1:T(8,128)S(1)} %copy-done.2, f32[1536,2,128]{0,2,1:T(8,128)S(1)} %fusion.11), kind=kLoop, calls=%fused_computation | loop fusion | flops 4718592 | bytes 10223616 | tf_op jit(solution)/shard_map/convert_element_type | solution.py:106
  143.8 3.1 %fusion.79 = f32[1536,512]{1,0:T(8,128)} fusion(bf16[1536,768]{0,1:T(8,128)(2,1)S(1)} %bitcast.49, bf16[768,512]{1,0:T(8,128)(2,1)S(1)} %bitcast.50), kind=kOutput, calls=%fused_computation.120 | convolution fusion | flops 1207959552 | bytes 6291456 | tf_op jit(solution)/shard_map/dot_general | solution.py:108
  147.0 63.6 %reduce-scatter.2.cloned.1.call-done = f32[96,512]{1,0:T(8,128)} async-done(((f32[1536,512]{1,0:T(8,128)}), f32[96,512]{1,0:T(8,128)}) %reduce-scatter.2.cloned.1.call-update) | async-done | bytes 196624 | tf_op jit(solution)/shard_map/reduce_scatter | solution.py:107
  210.6 1.1 fusion.74
  211.7 1.7 fusion.77
  (41 shorter events, 1.8 us)
Async XLA Ops:
  6.5 2.5 %copy-start = (bf16[1,1024,1024]{2,1,0:T(8,128)(2,1)S(1)}, bf16[1,1024,1024]{2,1,0:T(8,128)(2,1)}, u32[]{:S(2)}) copy-start(bf16[1,1024,1024]{2,1,0:T(8,128)(2,1)} %param.8) | copy-start | bytes 6291460
  6.5 48.2 %all-reduce.2.cloned.1.call-start = ((), (), s32[]{:S(2)}) async-start(), calls=%async_computation.1 | async-start | bytes 393216 | tf_op jit(solution)/shard_map/psum | solution.py:25
  9.1 17.1 %copy-start.8 = (f32[1,1024]{1,0:T(1,128)S(1)}, f32[1,1024]{1,0:T(1,128)}, u32[]{:S(2)}) copy-start(f32[1,1024]{1,0:T(1,128)} %param.9) | copy-start | bytes 12292
  12.5 13.2 %collective-permute-start = (bf16[192,1024]{1,0:T(8,128)(2,1)S(1)}, bf16[192,1024]{1,0:T(8,128)(2,1)S(1)}, u32[]{:S(2)}, u32[]{:S(2)}) collective-permute-start(bf16[192,1024]{1,0:T(8,128)(2,1)S(1)} %fusion.31), channel_id=1, source_target_pairs={{0,16},{1,17},{2,18},{3,19},{4,20},{5,21},{6,22},{7,23},{8,24},{9,... | collective-permute-start | bytes 1179656 | tf_op jit(solution)/shard_map/ppermute | solution.py:20
  26.2 2.7 %copy-start.7 = (bf16[1024,512]{1,0:T(8,128)(2,1)S(1)}, bf16[1024,512]{1,0:T(8,128)(2,1)}, u32[]{:S(2)}) copy-start(bf16[1024,512]{1,0:T(8,128)(2,1)} %param.10) | copy-start | bytes 3145732
  28.6 28.9 %copy-start.6 = (s32[1,96]{1,0:T(1,128)S(1)}, s32[1,96]{1,0:T(1,128)}, u32[]{:S(2)}) copy-start(s32[1,96]{1,0:T(1,128)} %param.13) | copy-start | bytes 1156
  28.6 51.3 %copy-start.3 = (bf16[1,2,3,128,512]{4,3,2,1,0:T(8,128)(2,1)S(1)}, bf16[1,2,3,128,512]{4,3,2,1,0:T(8,128)(2,1)}, u32[]{:S(2)}) copy-start(bf16[1,2,3,128,512]{4,3,2,1,0:T(8,128)(2,1)} %param.11) | copy-start | bytes 2359300
  28.9 51.2 %copy-start.9 = (s32[1,2]{1,0:T(1,128)S(1)}, s32[1,2]{1,0:T(1,128)}, u32[]{:S(2)}) copy-start(s32[1,2]{1,0:T(1,128)} %param.12) | copy-start | bytes 28
  30.1 67.2 %all-gather.4.cloned.1.call-start = ((), (), s32[]{:S(2)}) async-start(), calls=%async_computation.3 | async-start | bytes 1671168 | tf_op jit(solution)/shard_map/all_gather | solution.py:72
  57.4 153.2 %reduce-scatter.2.cloned.1.call-start = ((), (), s32[]{:S(2)}) async-start(), calls=%async_computation.2 | async-start | bytes 3342336 | tf_op jit(solution)/shard_map/reduce_scatter | solution.py:107
  102.6 1.2 copy-start.1
  137.2 3.2 %copy-start.2 = (f32[1536,2,128]{0,2,1:T(8,128)S(1)}, f32[1536,2,128]{0,2,1:T(8,128)}, u32[]{:S(2)}) copy-start(f32[1536,2,128]{0,2,1:T(8,128)} %copy-done.1) | copy-start | bytes 4718596
  140.4 3.5 %copy-start.4 = (bf16[1,2,3,128,512]{4,3,2,1,0:T(8,128)(2,1)S(1)}, bf16[1,2,3,128,512]{4,3,2,1,0:T(8,128)(2,1)}, u32[]{:S(2)}) copy-start(bf16[1,2,3,128,512]{4,3,2,1,0:T(8,128)(2,1)} %fusion.6) | copy-start | bytes 2359300
  146.9 63.6 %copy-start.5 = (bf16[192,512]{1,0:T(8,128)(2,1)S(1)}, bf16[192,512]{1,0:T(8,128)(2,1)}, u32[]{:S(2)}) copy-start(bf16[192,512]{1,0:T(8,128)(2,1)} %all-reduce.2.cloned.1.call-done) | copy-start | bytes 589828
Sparse Core Ops, SparseCore 0:
  30.2 24.5 all-reduce.1
  57.5 39.6 all-gather.3
  147.1 63.4 reduce-scatter.1
where the time goes:
time: 220 us
  waiting for transfers between devices  112 us (51%)
  blocking collectives  53.5 us (24%)
  other arithmetic  18.5 us (8%)
  matrix products  15.4 us (7%)
  between operations  13.3 us (6%)
  starting transfers between devices  4.98 us (2%)
    reduce_scatter x1, waiting for transfers between devices, shards(): lax.psum_scatter(jnp.dot(pulled, unit_centers, preferred_element_type=jnp...  63.6 us
    psum x1, blocking collectives, shards(): totals = lax.psum(jnp.sum(exp_logits, axis=(1, 2)), 'ident')  32.3 us
    psum x1, waiting for transfers between devices, broadcast(): return lax.psum(block, axis)  24.6 us
    all_gather x1, blocking collectives, shards(): lax.all_gather(labels, 'ident', axis=0, tiled=True)  21.2 us
    all_gather x1, waiting for transfers between devices, shards(): lax.all_gather(unit_own[None], 'ident', axis=0, tiled=True)  15.9 us
    ppermute x1, waiting for transfers between devices, from_behind(): return lax.ppermute(block, axis, route)  8.32 us
    dot_general x2, matrix products, section_apply(): mixed = jnp.dot(normed, weight, preferred_element_type=jnp.float32)  5.85 us
    dot_general x1, matrix products, shards(): lax.dot_general(feature, unit_centers, (((1,), (1,)), ((), ())), preferre...  5.35 us
  transfers between devices with their start and end apart: 4, of which 4 were waited for; matrix products, arithmetic and copies ran while one was open for 1% of the time, Pallas kernels for 0%

commit v1 on v0

v1 whole, which is shorter than its diff:
```python
import functools
import math

import jax
import jax.numpy as jnp
from jax import lax
from jax.experimental import pallas as pl
from jax.experimental.pallas import tpu as pltpu
from jax.sharding import PartitionSpec as P

BLOCKS_DEV = 256

logit_scale = 64.0
pool_temp = 0.1
margin_angle = 0.5
sine_offset = 1.05

MESH = pl.DeviceIdType.MESH


def split_of(count):
    cores = 2 if count % 2 == 0 else 1
    chips = count // cores
    x = 1
    while (2 * x) * (2 * x) <= chips and chips % (2 * x) == 0:
        x *= 2
    return chips // x, x, cores


def layer_norm(valf):
    center = valf - jnp.mean(valf, axis=-1, keepdims=True)
    spread = jnp.mean(center * center, axis=-1, keepdims=True)
    return center * lax.rsqrt(spread + 1e-06)


def kernel(
    sections, Z, X, C,
    trunk_hbm, weight_hbm, gain_ref, neck_hbm, centers_hbm, sampled_ref, labels_ref,
    out_ref,
    trunk, weight, neck, centers, unit, hid_out, emb_send, emb, feats, labs, lab_tmp,
    expo, coef_a, coef_b, tparts, tsum, pulled, gown, gsend, recv_t, send_x, recv_x, send_z, recv_z,
    local_sem, hid_send_sem, hid_recv_sem, emb_send_sem, emb_recv_sem,
    lab_send_sem, lab_recv_sem, t_send_sem, t_recv_sem,
    fz_send_sem, fx_send_sem, fc_send_sem, f_recv_sem,
    gc_send_sem, gc_recv_sem, gx_send_sem, gx_recv_sem, gz_send_sem, gz_recv_sem,
):
    n = Z * X * C
    pair = 2 if Z % 2 == 0 else 1
    NP = Z // pair
    G = pair * C
    s = lax.axis_index("section")
    me = lax.axis_index("ident")
    c = lax.rem(me, C)
    x = lax.rem(me // C, X)
    z = me // (C * X)
    rows, width = emb.shape
    nsamp, nsub, nblk = expo.shape[1], expo.shape[2], expo.shape[3]
    lanes = G * rows

    def ident_of(zz, xx, cc):
        return (zz * X + xx) * C + cc

    def slot_of(zz, xx, cc):
        return (xx * Z + zz) * C + cc

    in_copy = pltpu.make_async_copy(trunk_hbm, trunk, local_sem.at[0])
    weight_copy = pltpu.make_async_copy(weight_hbm, weight, local_sem.at[1])
    neck_copy = pltpu.make_async_copy(neck_hbm, neck, local_sem.at[2])
    centers_copy = pltpu.make_async_copy(centers_hbm, centers, local_sem.at[3])

    @pl.when(s == 0)
    def _():
        in_copy.start()

    weight_copy.start()

    @pl.when(s == sections - 1)
    def _():
        neck_copy.start()

    centers_copy.start()

    barrier = pltpu.get_barrier_semaphore()

    @pl.loop(1, n)
    def _(d):
        pl.semaphore_signal(
            barrier, inc=1, device_id=(s, lax.rem(me + d, n)), device_id_type=MESH
        )

    for d in range(1, sections):
        pl.semaphore_signal(
            barrier, inc=1, device_id=(lax.rem(s + d, sections), me), device_id_type=MESH
        )

    place = lax.rem(z, pair) * C + c
    lab_tmp[...] = jnp.zeros_like(lab_tmp)
    lab_tmp[0:1, 0:rows] = labels_ref[...]
    labs[me] = pltpu.roll(lab_tmp[...], place * rows, 1)

    pl.semaphore_wait(barrier, n - 1 + sections - 1)

    def lab_copy(peer, index):
        return pltpu.make_async_remote_copy(
            src_ref=labs.at[me], dst_ref=labs.at[me],
            send_sem=lab_send_sem.at[index], recv_sem=lab_recv_sem.at[me],
            device_id=(s, peer), device_id_type=MESH,
        )

    def prepare_centers():
        centers_copy.wait()
        step = 64

        @pl.loop(0, centers.shape[0] // step)
        def _(i):
            at = pl.ds(pl.multiple_of(i * step, step), step)
            valf = centers[at, :].astype(jnp.float32)
            inv = lax.rsqrt(jnp.sum(valf * valf, axis=-1, keepdims=True) + 1e-06)
            unit[at, :] = (valf * inv).astype(jnp.bfloat16)

    def send_labels():
        @pl.loop(1, n)
        def _(d):
            lab_copy(lax.rem(me + d, n), d).start()

    @pl.when(s > 0)
    def _():
        send_labels()
        prepare_centers()

    weight_copy.wait()

    @pl.when(s == 0)
    def _():
        in_copy.wait()

    @pl.when(s == sections - 1)
    def _():
        neck_copy.wait()

    def hid_copy(j):
        return pltpu.make_async_remote_copy(
            src_ref=hid_out.at[j], dst_ref=trunk.at[j],
            send_sem=hid_send_sem.at[j], recv_sem=hid_recv_sem.at[j],
            device_id=(lax.rem(s + 1, sections), me), device_id_type=MESH,
        )

    def emb_copy(j):
        return pltpu.make_async_remote_copy(
            src_ref=emb_send.at[j], dst_ref=emb,
            send_sem=emb_send_sem.at[j], recv_sem=emb_recv_sem,
            device_id=(j, me), device_id_type=MESH,
        )

    for j in range(sections):
        @pl.when(s > 0)
        def _():
            hid_copy(j).wait_recv()

        valf = trunk[j].astype(jnp.float32)
        normed = (layer_norm(valf) * gain_ref[...]).astype(jnp.bfloat16)
        mixed = jnp.dot(normed, weight[...], preferred_element_type=jnp.float32)
        act = mixed * (lax.erf(mixed * (1.0 / math.sqrt(2.0))) + 1.0) * 0.5
        hid_out[j] = (valf + act).astype(jnp.bfloat16)

        @pl.when(s < sections - 1)
        def _():
            hid_copy(j).start()

        @pl.when(s == sections - 1)
        def _():
            neck_in = layer_norm(hid_out[j].astype(jnp.float32)).astype(jnp.bfloat16)
            embed = jnp.dot(neck_in, neck[...], preferred_element_type=jnp.float32)
            if j == sections - 1:
                emb[...] = embed.astype(jnp.bfloat16)
            else:
                emb_send[j] = embed.astype(jnp.bfloat16)
                emb_copy(j).start()

    @pl.when(s == 0)
    def _():
        send_labels()
        prepare_centers()

    @pl.when(s < sections - 1)
    def _():
        emb_copy(0).wait_recv()

    valf = emb[...].astype(jnp.float32)
    inverse = lax.rsqrt(jnp.sum(valf * valf, axis=-1, keepdims=True) + 1e-06)
    feats[slot_of(z, x, c)] = (valf * inverse).astype(jnp.bfloat16)

    def push(slot, send_sem, device):
        return pltpu.make_async_remote_copy(
            src_ref=feats.at[slot], dst_ref=feats.at[slot],
            send_sem=send_sem, recv_sem=f_recv_sem.at[slot],
            device_id=(s, device), device_id_type=MESH,
        )

    def z_send(d):
        zz = lax.rem(z + d, Z)
        return push(slot_of(z, x, c), fz_send_sem.at[d], ident_of(zz, x, c))

    def x_send(zz, d):
        xx = lax.rem(x + d, X)
        return push(slot_of(zz, x, c), fx_send_sem.at[zz, d], ident_of(z, xx, c))

    def c_send(zz, xx, d):
        cc = lax.rem(c + d, C)
        return push(slot_of(zz, xx, c), fc_send_sem.at[xx * Z + zz, d], ident_of(z, x, cc))

    def arrived(zz, xx, cc):
        push(slot_of(zz, xx, cc), fz_send_sem.at[0], me).wait_recv()

    def others(p, first):
        base = lax.rem(z // pair + p, NP) * pair
        return [base + lax.rem(lax.rem(z, pair) + j, pair) for j in range(pair)][first:]

    for d in range(1, Z):
        z_send(d).start()
    for d in range(1, X):
        x_send(z, d).start()
    for d in range(1, C):
        c_send(z, x, d).start()

    lane_index = lax.broadcasted_iota(jnp.int32, (16, lanes), 0)
    cos_m, sin_m = math.cos(margin_angle), math.sin(margin_angle)

    def forward_scores(p, xx):
        pr = lax.rem(z // pair + p, NP)
        ch = xx * NP + pr
        block = feats[pl.ds(ch * G, G)].reshape(lanes, width)
        lab = None
        for j in range(pair):
            for cc in range(C):
                one = labs[ident_of(pr * pair + j, xx, cc)]
                lab = one if lab is None else lab + one
        lab = jnp.broadcast_to(lab[0:1], (16, lanes))
        total = jnp.zeros((16, lanes), jnp.float32)
        for a in range(nsamp):
            cosines = []
            for k in range(nsub):
                cosines.append(lax.dot_general(
                    unit[(a * nsub + k) * nblk:(a * nsub + k + 1) * nblk, :], block,
                    (((1,), (1,)), ((), ())), preferred_element_type=jnp.float32,
                ))
            first = me * (BLOCKS_DEV * nblk) + sampled_ref[0, a] * nblk
            for r in range(0, nblk, 16):
                exps = [jnp.exp(cosines[k][r:r + 16] * (1.0 / pool_temp)) for k in range(nsub)]
                summed = exps[0]
                for k in range(1, nsub):
                    summed = summed + exps[k]
                pooled = pool_temp * jnp.log(summed * (1.0 / nsub))
                target = lab == (first + r + lane_index)
                gap = sine_offset - pooled * pooled
                rroot = lax.rsqrt(gap)
                logits = logit_scale * jnp.where(
                    target, pooled * cos_m - gap * rroot * sin_m, pooled
                )
                slope = jnp.where(target, cos_m + pooled * sin_m * rroot, 1.0)
                el = jnp.exp(logits)
                total = total + el
                scaled = logit_scale * slope / summed
                at = slice(r, r + 16)
                coef_a[ch, a, at, :] = el * scaled
                coef_b[ch, a, at, :] = jnp.where(target, scaled, 0.0)
                for k in range(nsub):
                    expo[ch, a, k, at, :] = exps[k].astype(expo.dtype)
        tparts[me, ch] = jnp.sum(total, axis=0, keepdims=True)

    def lab_wait():
        @pl.loop(1, n)
        def _(d):
            peer = lax.rem(me + d, n)
            pltpu.make_async_remote_copy(
                src_ref=labs.at[peer], dst_ref=labs.at[peer],
                send_sem=lab_send_sem.at[0], recv_sem=lab_recv_sem.at[peer],
                device_id=(s, peer), device_id_type=MESH,
            ).wait_recv()

    lab_wait()
    for p in range(NP):
        for zz in others(p, 1 if p == 0 else 0):
            arrived(zz, x, c)
            for d in range(1, X):
                x_send(zz, d).start()
            for d in range(1, C):
                c_send(zz, x, d).start()
        for zz in others(p, 0):
            for d in range(1, C):
                arrived(zz, x, lax.rem(c + d, C))
        forward_scores(p, x)
    for dx in range(1, X):
        xx = lax.rem(x + dx, X)
        for p in range(NP):
            for zz in others(p, 0):
                arrived(zz, xx, c)
                for d in range(1, C):
                    c_send(zz, xx, d).start()
            for zz in others(p, 0):
                for d in range(1, C):
                    arrived(zz, xx, lax.rem(c + d, C))
            forward_scores(p, xx)

    def t_copy(src, peer, index):
        return pltpu.make_async_remote_copy(
            src_ref=tparts.at[src], dst_ref=tparts.at[src],
            send_sem=t_send_sem.at[index], recv_sem=t_recv_sem.at[src],
            device_id=(s, peer), device_id_type=MESH,
        )

    @pl.loop(1, n)
    def _(d):
        t_copy(me, lax.rem(me + d, n), d).start()

    @pl.loop(1, n)
    def _(d):
        peer = lax.rem(me + d, n)
        t_copy(peer, peer, 0).wait_recv()

    tsum[...] = 1.0 / jnp.sum(tparts[...], axis=0)

    def gc_copy(zz, xx, d):
        cc = lax.rem(c + d, C)
        return pltpu.make_async_remote_copy(
            src_ref=gsend.at[slot_of(zz, xx, cc)], dst_ref=recv_t.at[xx * Z + zz, c],
            send_sem=gc_send_sem.at[slot_of(zz, xx, cc)], recv_sem=gc_recv_sem.at[xx * Z + zz, c],
            device_id=(s, ident_of(z, x, cc)), device_id_type=MESH,
        )

    def gc_arrived(zz, xx, cc):
        pltpu.make_async_remote_copy(
            src_ref=recv_t.at[xx * Z + zz, cc], dst_ref=recv_t.at[xx * Z + zz, cc],
            send_sem=gc_send_sem.at[0], recv_sem=gc_recv_sem.at[xx * Z + zz, cc],
            device_id=(s, me), device_id_type=MESH,
        ).wait_recv()

    def gx_copy(zz, xx):
        return pltpu.make_async_remote_copy(
            src_ref=send_x.at[xx * Z + zz], dst_ref=recv_x.at[x * Z + zz],
            send_sem=gx_send_sem.at[xx * Z + zz], recv_sem=gx_recv_sem.at[x * Z + zz],
            device_id=(s, ident_of(z, xx, c)), device_id_type=MESH,
        )

    def gz_copy(zz):
        return pltpu.make_async_remote_copy(
            src_ref=send_z.at[zz], dst_ref=recv_z.at[z],
            send_sem=gz_send_sem.at[zz], recv_sem=gz_recv_sem.at[z],
            device_id=(s, ident_of(zz, x, c)), device_id_type=MESH,
        )

    def backward(p, xx):
        pr = lax.rem(z // pair + p, NP)
        ch = xx * NP + pr
        inv_total = jnp.broadcast_to(tsum[ch], (16, lanes))
        for a in range(nsamp):
            for r in range(0, nblk, 16):
                at = slice(r, r + 16)
                factor = coef_a[ch, a, at, :] * inv_total - coef_b[ch, a, at, :]
                for k in range(nsub):
                    first = (a * nsub + k) * nblk + r
                    pulled[first:first + 16, :] = (
                        factor * expo[ch, a, k, at, :].astype(jnp.float32)
                    ).astype(jnp.bfloat16)
        grad = lax.dot_general(
            pulled[...], unit[...], (((0,), (0,)), ((), ())), preferred_element_type=jnp.float32
        ).reshape(G, rows, width)
        gown[pl.ds(ch * G, G)] = grad
        gsend[pl.ds(ch * G, G)] = grad.astype(jnp.bfloat16)
        for zz in others(p, 0):
            for d in range(1, C):
                gc_copy(zz, xx, d).start()

    def core_sum(zz, xx):
        value = gown[slot_of(zz, xx, c)]
        for d in range(1, C):
            cc = lax.rem(c + d, C)
            gc_arrived(zz, xx, cc)
            value = value + recv_t[xx * Z + zz, cc].astype(jnp.float32)
        return value

    def reduce_step(p, dx):
        if dx:
            xx = lax.rem(x + dx, X)
            for zz in others(p, 0):
                send_x[xx * Z + zz] = core_sum(zz, xx).astype(jnp.bfloat16)
                gx_copy(zz, xx).start()
            return None
        mine = None
        order = others(p, 0)
        for zz in (order[1:] + order[:1]) if p == 0 else order:
            value = core_sum(zz, x)
            for d in range(1, X):
                xx = lax.rem(x + d, X)
                pltpu.make_async_remote_copy(
                    src_ref=send_x.at[xx * Z + zz], dst_ref=recv_x.at[xx * Z + zz],
                    send_sem=gx_send_sem.at[xx * Z + zz], recv_sem=gx_recv_sem.at[xx * Z + zz],
                    device_id=(s, me), device_id_type=MESH,
                ).wait_recv()
                value = value + recv_x[xx * Z + zz].astype(jnp.float32)
            if p == 0 and zz is order[0]:
                mine = value
            else:
                send_z[zz] = value.astype(jnp.bfloat16)
                gz_copy(zz).start()
        return mine

    plan = [(p, dx) for dx in list(range(1, X)) + [0] for p in reversed(range(NP))]
    for i, (p, dx) in enumerate(plan):
        backward(p, lax.rem(x + dx, X))
        if i:
            reduce_step(*plan[i - 1])
    own_grad = reduce_step(*plan[-1])

    for d in range(1, Z):
        zz = lax.rem(z + d, Z)
        pltpu.make_async_remote_copy(
            src_ref=send_z.at[zz], dst_ref=recv_z.at[zz],
            send_sem=gz_send_sem.at[zz], recv_sem=gz_recv_sem.at[zz],
            device_id=(s, me), device_id_type=MESH,
        ).wait_recv()
        own_grad = own_grad + recv_z[zz].astype(jnp.float32)

    valf = emb[...].astype(jnp.float32)
    inverse = lax.rsqrt(jnp.sum(valf * valf, axis=-1, keepdims=True) + 1e-06)
    direction = valf * inverse
    along = jnp.sum(own_grad * direction, axis=-1, keepdims=True)
    out_ref[0] = inverse * (own_grad - along * direction)

    for j in range(sections):
        @pl.when(s < sections - 1)
        def _():
            hid_copy(j).wait_send()

        if j < sections - 1:
            @pl.when(s == sections - 1)
            def _():
                emb_copy(j).wait_send()

    @pl.loop(1, n)
    def _(d):
        lab_copy(lax.rem(me + d, n), d).wait_send()
        t_copy(me, lax.rem(me + d, n), d).wait_send()

    for d in range(1, Z):
        z_send(d).wait_send()
    for j in range(Z):
        zz = lax.rem(z + j, Z)
        for d in range(1, X):
            x_send(zz, d).wait_send()
            gx_copy(zz, lax.rem(x + d, X)).wait_send()
        if j:
            gz_copy(zz).wait_send()
        for i in range(X):
            for d in range(1, C):
                c_send(zz, lax.rem(x + i, X), d).wait_send()
                gc_copy(zz, lax.rem(x + i, X), d).wait_send()


def shards(Z, X, C, inputs, section_weight, section_gain, neck_weight, centers, sampled, labels):
    sections = lax.axis_size("section")
    n = Z * X * C
    dim = inputs.shape[-1]
    rows = inputs.shape[1] // sections
    _, nsamp, nsub, nblk, width = centers.shape
    pair = 2 if Z % 2 == 0 else 1
    group = pair * C
    chunks = n // group
    lanes = group * rows
    total_rows = n * rows
    bf16, f32 = jnp.bfloat16, jnp.float32
    expo_type = f32 if total_rows * nsamp * nsub * nblk * 4 <= 8 * 2**20 else bf16
    dma = pltpu.SemaphoreType.DMA
    vmem = pltpu.VMEM
    flat = centers.reshape(-1, width)
    scratch = [
        vmem((sections, rows, dim), bf16),
        vmem(section_weight.shape[1:], bf16),
        vmem(neck_weight.shape, bf16),
        vmem(flat.shape, bf16),
        vmem(flat.shape, bf16),
        vmem((sections, rows, dim), bf16),
        vmem((sections, rows, width), bf16),
        vmem((rows, width), bf16),
        vmem((n, rows, width), bf16),
        vmem((n, 8, lanes), jnp.int32),
        vmem((8, lanes), jnp.int32),
        vmem((chunks, nsamp, nsub, nblk, lanes), expo_type),
        vmem((chunks, nsamp, nblk, lanes), f32),
        vmem((chunks, nsamp, nblk, lanes), f32),
        vmem((n, chunks, 1, lanes), f32),
        vmem((chunks, 1, lanes), f32),
        vmem((nsamp * nsub * nblk, lanes), bf16),
        vmem((n, rows, width), f32),
        vmem((n, rows, width), bf16),
        vmem((X * Z, C, rows, width), bf16),
        vmem((X * Z, rows, width), bf16),
        vmem((X * Z, rows, width), bf16),
        vmem((Z, rows, width), bf16),
        vmem((Z, rows, width), bf16),
        dma((4,)), dma((sections,)), dma((sections,)), dma((sections,)), dma,
        dma((n,)), dma((n,)), dma((n,)), dma((n,)),
        dma((Z,)), dma((Z, X)), dma((X * Z, C)), dma((n,)),
        dma((n,)), dma((X * Z, C)), dma((X * Z,)), dma((X * Z,)), dma((Z,)), dma((Z,)),
    ]
    any_spec = pl.BlockSpec(memory_space=pl.ANY)
    vmem_spec = pl.BlockSpec(memory_space=pltpu.VMEM)
    smem_spec = pl.BlockSpec(memory_space=pltpu.SMEM)
    return pl.pallas_call(
        functools.partial(kernel, sections, Z, X, C),
        out_shape=jax.ShapeDtypeStruct((1, rows, width), f32),
        in_specs=[any_spec, any_spec, vmem_spec, any_spec, any_spec, smem_spec, vmem_spec],
        out_specs=vmem_spec,
        scratch_shapes=scratch,
        compiler_params=pltpu.CompilerParams(
            collective_id=0, has_side_effects=True, vmem_limit_bytes=62 * 2**20
        ),
        name="arcface_head",
    )(
        inputs.reshape(sections, rows, dim), section_weight[0], section_gain, neck_weight,
        flat, sampled, labels,
    )


def solution(mesh):
    Z, X, C = split_of(mesh.shape["ident"])
    in_specs = (
        P("ident", None, None),
        P("section", None, None),
        P("section", None),
        P(),
        P("ident", None, None, None, None),
        P("ident", None),
        P("ident", "section"),
    )
    out_specs = P("ident", "section", None)
    return jax.shard_map(
        functools.partial(shards, Z, X, C),
        mesh=mesh, in_specs=in_specs, out_specs=out_specs, check_vma=False,
    )
```

time: 220 us -> 59.4 us (0.27)
  waiting for transfers between devices: 112 us -> 0 us
  Pallas kernels: 0 us -> 57.6 us
  blocking collectives: 53.5 us -> 0 us
  other arithmetic: 18.5 us -> 0 us
  matrix products: 15.4 us -> 0 us
  between operations: 13.3 us -> 0.01 us
  starting transfers between devices: 4.98 us -> 0 us
    reduce_scatter x1 -> x0, waiting for transfers between devices: 63.6 us -> none  [shards(): lax.psum_scatter(jnp.dot(pulled, unit_centers, preferred_element_type=jnp...]
    pallas_call x0 -> x1, Pallas kernels: none -> 57.6 us  [shards(): pl.pallas_call(functools.partial(kernel, sections, Z, X, C), out_shape=ja...]
    psum x1 -> x0, blocking collectives: 32.3 us -> none  [shards(): totals = lax.psum(jnp.sum(exp_logits, axis=(1, 2)), 'ident')]
    psum x1 -> x0, waiting for transfers between devices: 24.6 us -> none  [broadcast(): return lax.psum(block, axis)]
    all_gather x1 -> x0, blocking collectives: 21.2 us -> none  [shards(): lax.all_gather(labels, 'ident', axis=0, tiled=True)]
    all_gather x1 -> x0, waiting for transfers between devices: 15.9 us -> none  [shards(): lax.all_gather(unit_own[None], 'ident', axis=0, tiled=True)]
    dot_general x5 -> x0, matrix products: 15.4 us -> none  [the longest x2 5.85 us: section_apply(): mixed = jnp.dot(normed, weight, preferred_element_type=jnp.float32)]
    ppermute x1 -> x0, waiting for transfers between devices: 8.32 us -> none  [from_behind(): return lax.ppermute(block, axis, route)]
  transfers between devices with their start and end apart: 4 -> 0, of which waited for: 4 -> 0; matrix products, arithmetic and copies ran while one was open for 1% -> 0% of each run, Pallas kernels for 0% -> 0%
where the time goes in v1:
time: 59.4 us; the launch traced here: 59.3 us
  Pallas kernels  57.6 us (97%)
  local copies, waits for them, and re-layouts  1.62 us (3%)
    pallas_call x1, Pallas kernels, shards(): pl.pallas_call(functools.partial(kernel, sections, Z, X, C), out_shape=ja...  57.6 us
    unnamed x1, local copies, waits for them, and re-layouts  1.62 us

profile of v1, /device:TPU:0, one launch (start us, length us, event | category | flops | bytes accessed | tf_op | source)
XLA Modules:
  0.0 59.3 jit_solution(11061291499661338237)
XLA Ops:
  0.0 57.6 %arcface_head.1 = f32[1,96,512]{2,1,0:T(8,128)} custom-call(bf16[2,96,1024]{2,1,0:T(8,128)(2,1)} %bitcast.5, bf16[1024,1024]{1,0:T(8,128)(2,1)} %bitcast.3, f32[1,1024]{1,0:T(1,128)} %gain_ref.1, bf16[1024,512]{1,0:T(8,128)(2,1)} %neck_hbm.1, bf16[768,512]{1,0:T(8,128)(2,1)} %bitcast.4, s32[1,2]{1,0:T(1,128)} %sampled_ref.1, s32[1,96]{1,0:T(1,128)} %labels_ref.1), custom_call_target="tpu_custom_call" | custom-call | tf_op jit(solution)/shard_map/arcface_head/pallas_call | solution.py:509
  57.6 1.6 %copy.9 = f32[1,96,512]{2,1,0:T(8,128)} copy(f32[1,96,512]{2,1,0:T(8,128)} %arcface_head.1) | data formatting | bytes 393216

commit v2 on v0

v2 whole, which is shorter than its diff:
```python
import functools
import math

import jax
import jax.numpy as jnp
from jax import lax
from jax.experimental import pallas as pl
from jax.experimental.pallas import tpu as pltpu
from jax.sharding import PartitionSpec as P

BLOCKS_DEV = 256

logit_scale = 64.0
pool_temp = 0.1
margin_angle = 0.5
sine_offset = 1.05

MESH = pl.DeviceIdType.MESH


def split_of(count):
    cores = 2 if count % 2 == 0 else 1
    chips = count // cores
    x = 1
    while (2 * x) * (2 * x) <= chips and chips % (2 * x) == 0:
        x *= 2
    return chips // x, x, cores


def layer_norm(valf):
    center = valf - jnp.mean(valf, axis=-1, keepdims=True)
    spread = jnp.mean(center * center, axis=-1, keepdims=True)
    return center * lax.rsqrt(spread + 1e-06)


def kernel(
    sections, Z, X, C,
    trunk_hbm, weight_hbm, gain_ref, neck_hbm, centers_hbm, sampled_ref, labels_ref,
    out_ref,
    trunk, weight, neck, raw, unit, hid_out, emb_send, emb, feats, labs, idents,
    expo, coef_a, coef_b, tparts, tsum, pulled, send_z, recv_z,
    local_sem, hid_send_sem, hid_recv_sem, emb_send_sem, emb_recv_sem,
    id_send_sem, id_recv_sem, lab_send_sem, lab_recv_sem, t_send_sem, t_recv_sem,
    rx_send_sem, rc_send_sem, r_recv_sem, f_send_sem, f_recv_sem, g_send_sem, g_recv_sem,
):
    Q = X * C
    s = lax.axis_index("section")
    me = lax.axis_index("ident")
    c = lax.rem(me, C)
    x = lax.rem(me // C, X)
    z = me // Q
    mine = x * C + c
    rows, width = emb.shape
    lanes = feats.shape[1]
    nsamp, nsub, nblk = expo.shape[2], expo.shape[3], expo.shape[4]
    per_slot = nsub * nblk

    def in_row(q):
        return (s, z * Q + q)

    def at_z(zz):
        return (s, zz * Q + mine)

    def remote(src, dst, send_sem, recv_sem, device):
        return pltpu.make_async_remote_copy(
            src_ref=src, dst_ref=dst, send_sem=send_sem, recv_sem=recv_sem,
            device_id=device, device_id_type=MESH,
        )

    in_copy = pltpu.make_async_copy(trunk_hbm, trunk, local_sem.at[0])
    weight_copy = pltpu.make_async_copy(weight_hbm, weight, local_sem.at[1])
    neck_copy = pltpu.make_async_copy(neck_hbm, neck, local_sem.at[2])
    centers_copy = pltpu.make_async_copy(centers_hbm, raw.at[mine], local_sem.at[3])

    @pl.when(s == 0)
    def _():
        in_copy.start()

    weight_copy.start()

    @pl.when(s == sections - 1)
    def _():
        neck_copy.start()

    centers_copy.start()

    if lanes > rows:
        feats[:, rows:lanes, :] = jnp.zeros((Z, lanes - rows, width), jnp.bfloat16)

    barrier = pltpu.get_barrier_semaphore()
    for d in range(1, Z):
        pl.semaphore_signal(barrier, inc=1, device_id=at_z(lax.rem(z + d, Z)), device_id_type=MESH)
    for d in range(1, Q):
        pl.semaphore_signal(barrier, inc=1, device_id=in_row(lax.rem(mine + d, Q)), device_id_type=MESH)
    for d in range(1, sections):
        pl.semaphore_signal(
            barrier, inc=1, device_id=(lax.rem(s + d, sections), me), device_id_type=MESH
        )

    labs[z] = jnp.full(labs.shape[1:], -1, jnp.int32)
    labs[z, 0:1, 0:rows] = labels_ref[...]
    for a in range(nsamp):
        first = me * (BLOCKS_DEV * nblk) + sampled_ref[0, a] * nblk
        idents[mine, a] = jnp.full((1, lanes), first, jnp.int32)

    pl.semaphore_wait(barrier, Z - 1 + Q - 1 + sections - 1)

    def half(a):
        return pl.ds(a * per_slot, per_slot)

    def rx_copy(d, a):
        xx = lax.rem(x + d, X)
        return remote(
            centers_hbm.at[half(a)], raw.at[mine, half(a)],
            rx_send_sem.at[d, a], r_recv_sem.at[mine, a], in_row(xx * C + c),
        )

    def rc_own(d, a):
        cc = lax.rem(c + d, C)
        return remote(
            centers_hbm.at[half(a)], raw.at[mine, half(a)],
            rc_send_sem.at[x, d, a], r_recv_sem.at[mine, a], in_row(x * C + cc),
        )

    def rc_forward(xx, d, a):
        cc = lax.rem(c + d, C)
        q = xx * C + c
        return remote(
            raw.at[q, half(a)], raw.at[q, half(a)],
            rc_send_sem.at[xx, d, a], r_recv_sem.at[q, a], in_row(x * C + cc),
        )

    def r_arrived(q, a):
        remote(
            raw.at[q, half(a)], raw.at[q, half(a)],
            rc_send_sem.at[0, 0, a], r_recv_sem.at[q, a], in_row(mine),
        ).wait_recv()

    def id_copy(src, q, index):
        return remote(
            idents.at[src], idents.at[src], id_send_sem.at[index], id_recv_sem.at[src], in_row(q)
        )

    def lab_copy(src, zz, index):
        return remote(
            labs.at[src], labs.at[src], lab_send_sem.at[index], lab_recv_sem.at[src], at_z(zz)
        )

    for a in range(nsamp):
        for d in range(1, X):
            rx_copy(d, a).start()
    for a in range(nsamp):
        for d in range(1, C):
            rc_own(d, a).start()
    for d in range(1, Q):
        id_copy(mine, lax.rem(mine + d, Q), d).start()
    for d in range(1, Z):
        lab_copy(z, lax.rem(z + d, Z), d).start()

    step = 64

    def prepare(q):
        @pl.loop(0, raw.shape[1] // step)
        def _(i):
            at = pl.ds(pl.multiple_of(i * step, step), step)
            valf = raw[q, at, :].astype(jnp.float32)
            inv = lax.rsqrt(jnp.sum(valf * valf, axis=-1, keepdims=True) + 1e-06)
            unit[q, at, :] = (valf * inv).astype(jnp.bfloat16)

    def prepare_chip():
        centers_copy.wait()
        prepare(mine)
        for d in range(1, C):
            q = x * C + lax.rem(c + d, C)
            for a in range(nsamp):
                r_arrived(q, a)
            prepare(q)

    @pl.when(s > 0)
    def _():
        prepare_chip()

    weight_copy.wait()

    @pl.when(s == 0)
    def _():
        in_copy.wait()

    @pl.when(s == sections - 1)
    def _():
        neck_copy.wait()

    def hid_copy(j):
        return remote(
            hid_out.at[j], trunk.at[j], hid_send_sem.at[j], hid_recv_sem.at[j],
            (lax.rem(s + 1, sections), me),
        )

    def emb_copy(j):
        return remote(emb_send.at[j], emb, emb_send_sem.at[j], emb_recv_sem, (j, me))

    for j in range(sections):
        @pl.when(s > 0)
        def _():
            hid_copy(j).wait_recv()

        valf = trunk[j].astype(jnp.float32)
        normed = (layer_norm(valf) * gain_ref[...]).astype(jnp.bfloat16)
        mixed = jnp.dot(normed, weight[...], preferred_element_type=jnp.float32)
        act = mixed * (lax.erf(mixed * (1.0 / math.sqrt(2.0))) + 1.0) * 0.5
        hid_out[j] = (valf + act).astype(jnp.bfloat16)

        @pl.when(s < sections - 1)
        def _():
            hid_copy(j).start()

        @pl.when(s == sections - 1)
        def _():
            neck_in = layer_norm(hid_out[j].astype(jnp.float32)).astype(jnp.bfloat16)
            embed = jnp.dot(neck_in, neck[...], preferred_element_type=jnp.float32)
            if j == sections - 1:
                emb[...] = embed.astype(jnp.bfloat16)
            else:
                emb_send[j] = embed.astype(jnp.bfloat16)
                emb_copy(j).start()

    @pl.when(s == 0)
    def _():
        prepare_chip()

    @pl.when(s < sections - 1)
    def _():
        emb_copy(0).wait_recv()

    valf = emb[...].astype(jnp.float32)
    inverse = lax.rsqrt(jnp.sum(valf * valf, axis=-1, keepdims=True) + 1e-06)
    feats[z, 0:rows, :] = (valf * inverse).astype(jnp.bfloat16)

    def near(k):
        high = (2 * z) // Z
        low = z + high * (Z - 1 - 2 * z)
        index = k + (k - low + Z) // Z
        return index + high * (Z - 1 - 2 * index)

    def f_copy(src, zz, index):
        part = feats.at[src, pl.ds(0, rows)]
        return remote(part, part, f_send_sem.at[index], f_recv_sem.at[src], at_z(zz))

    for k in range(Z - 1):
        f_copy(z, near(k), k).start()

    for d in range(1, X):
        xx = lax.rem(x + d, X)
        for a in range(nsamp):
            r_arrived(xx * C + c, a)
            for e in range(1, C):
                rc_forward(xx, e, a).start()
    for d in range(1, X):
        xx = lax.rem(x + d, X)
        prepare(xx * C + c)
    for d in range(1, X):
        xx = lax.rem(x + d, X)
        for e in range(1, C):
            q = xx * C + lax.rem(c + e, C)
            for a in range(nsamp):
                r_arrived(q, a)
            prepare(q)
    for d in range(1, Q):
        q = lax.rem(mine + d, Q)
        id_copy(q, q, 0).wait_recv()
    for k in range(Z - 1):
        lab_copy(near(k), near(k), 0).wait_recv()

    tile = 32
    row_index = lax.broadcasted_iota(jnp.int32, (tile, lanes), 0)
    cos_m, sin_m = math.cos(margin_angle), math.sin(margin_angle)

    def scores(zz):
        lab = jnp.broadcast_to(labs[zz, 0:1, :], (tile, lanes)) - row_index

        def shard(q, total):
            for a in range(nsamp):
                cosine = lax.dot_general(
                    unit[q, half(a), :], feats[zz],
                    (((1,), (1,)), ((), ())), preferred_element_type=jnp.float32,
                )
                hit = lab - jnp.broadcast_to(idents[q, a], (tile, lanes))
                for r in range(0, nblk, tile):
                    exps = [
                        jnp.exp(cosine[k * nblk + r:k * nblk + r + tile] * (1.0 / pool_temp))
                        for k in range(nsub)
                    ]
                    summed = exps[0]
                    for k in range(1, nsub):
                        summed = summed + exps[k]
                    pooled = pool_temp * jnp.log(summed * (1.0 / nsub))
                    target = hit == r
                    gap = sine_offset - pooled * pooled
                    rroot = lax.rsqrt(gap)
                    logits = logit_scale * jnp.where(
                        target, pooled * cos_m - gap * rroot * sin_m, pooled
                    )
                    slope = jnp.where(target, cos_m + pooled * sin_m * rroot, 1.0)
                    el = jnp.exp(logits)
                    total = total + el
                    scaled = logit_scale * slope / summed
                    at = slice(r, r + tile)
                    coef_a[zz, q, a, at, :] = el * scaled
                    coef_b[zz, q, a, at, :] = jnp.where(target, scaled, 0.0)
                    for k in range(nsub):
                        expo[zz, q, a, k, at, :] = exps[k].astype(expo.dtype)
            return total

        total = lax.fori_loop(0, Q, shard, jnp.zeros((tile, lanes), jnp.float32))
        tparts[z, zz] = jnp.sum(total, axis=0, keepdims=True)

    scores(z)
    for k in range(Z - 1):
        f_copy(near(k), near(k), 0).wait_recv()
        scores(near(k))

    def t_copy(src, zz, index):
        return remote(
            tparts.at[src], tparts.at[src], t_send_sem.at[index], t_recv_sem.at[src], at_z(zz)
        )

    for k in range(Z - 1):
        t_copy(z, near(k), k).start()
    for k in range(Z - 1):
        t_copy(near(k), near(k), 0).wait_recv()

    tsum[...] = 1.0 / jnp.sum(tparts[...], axis=0)

    def backward(zz):
        inv_total = jnp.broadcast_to(tsum[zz], (tile, lanes))

        @pl.loop(0, Q)
        def _(q):
            for a in range(nsamp):
                for r in range(0, nblk, tile):
                    at = slice(r, r + tile)
                    factor = coef_a[zz, q, a, at, :] * inv_total - coef_b[zz, q, a, at, :]
                    for k in range(nsub):
                        first = (a * nsub + k) * nblk + r
                        pulled[q, first:first + tile, :] = (
                            factor * expo[zz, q, a, k, at, :].astype(jnp.float32)
                        ).astype(jnp.bfloat16)

        grad = lax.dot_general(
            pulled[...].reshape(-1, lanes), unit[...].reshape(-1, width),
            (((0,), (0,)), ((), ())), preferred_element_type=jnp.float32,
        )
        return grad[0:rows]

    def g_copy(zz):
        return remote(
            send_z.at[zz], recv_z.at[z], g_send_sem.at[zz], g_recv_sem.at[z], at_z(zz)
        )

    for k in reversed(range(Z - 1)):
        send_z[near(k)] = backward(near(k)).astype(jnp.bfloat16)
        g_copy(near(k)).start()
    own_grad = backward(z)

    for k in range(Z - 1):
        zz = near(k)
        remote(
            send_z.at[zz], recv_z.at[zz], g_send_sem.at[zz], g_recv_sem.at[zz], at_z(zz)
        ).wait_recv()
        own_grad = own_grad + recv_z[zz].astype(jnp.float32)

    valf = emb[...].astype(jnp.float32)
    inverse = lax.rsqrt(jnp.sum(valf * valf, axis=-1, keepdims=True) + 1e-06)
    direction = valf * inverse
    along = jnp.sum(own_grad * direction, axis=-1, keepdims=True)
    out_ref[0] = inverse * (own_grad - along * direction)

    for j in range(sections):
        @pl.when(s < sections - 1)
        def _():
            hid_copy(j).wait_send()

        if j < sections - 1:
            @pl.when(s == sections - 1)
            def _():
                emb_copy(j).wait_send()

    for d in range(1, Q):
        id_copy(mine, lax.rem(mine + d, Q), d).wait_send()
    for d in range(1, Z):
        lab_copy(z, lax.rem(z + d, Z), d).wait_send()
    for a in range(nsamp):
        for d in range(1, X):
            rx_copy(d, a).wait_send()
            for e in range(1, C):
                rc_forward(lax.rem(x + d, X), e, a).wait_send()
        for d in range(1, C):
            rc_own(d, a).wait_send()
    for k in range(Z - 1):
        f_copy(z, near(k), k).wait_send()
        t_copy(z, near(k), k).wait_send()
        g_copy(near(k)).wait_send()


def shards(Z, X, C, inputs, section_weight, section_gain, neck_weight, centers, sampled, labels):
    sections = lax.axis_size("section")
    Q = X * C
    dim = inputs.shape[-1]
    rows = inputs.shape[1] // sections
    _, nsamp, nsub, nblk, width = centers.shape
    lanes = -(-rows // 128) * 128
    bf16, f32 = jnp.bfloat16, jnp.float32
    expo_type = f32 if Z * lanes * Q * nsamp * nsub * nblk * 4 <= 8 * 2**20 else bf16
    dma = pltpu.SemaphoreType.DMA
    vmem = pltpu.VMEM
    flat = centers.reshape(-1, width)
    scratch = [
        vmem((sections, rows, dim), bf16),
        vmem(section_weight.shape[1:], bf16),
        vmem(neck_weight.shape, bf16),
        vmem((Q,) + flat.shape, bf16),
        vmem((Q,) + flat.shape, bf16),
        vmem((sections, rows, dim), bf16),
        vmem((sections, rows, width), bf16),
        vmem((rows, width), bf16),
        vmem((Z, lanes, width), bf16),
        vmem((Z, 8, lanes), jnp.int32),
        vmem((Q, nsamp, 1, lanes), jnp.int32),
        vmem((Z, Q, nsamp, nsub, nblk, lanes), expo_type),
        vmem((Z, Q, nsamp, nblk, lanes), f32),
        vmem((Z, Q, nsamp, nblk, lanes), f32),
        vmem((Z, Z, 1, lanes), f32),
        vmem((Z, 1, lanes), f32),
        vmem((Q, nsamp * nsub * nblk, lanes), bf16),
        vmem((Z, rows, width), bf16),
        vmem((Z, rows, width), bf16),
        dma((4,)), dma((sections,)), dma((sections,)), dma((sections,)), dma,
        dma((Q,)), dma((Q,)), dma((Z,)), dma((Z,)), dma((Z,)), dma((Z,)),
        dma((X, nsamp)), dma((X, C, nsamp)), dma((Q, nsamp)), dma((Z,)), dma((Z,)),
        dma((Z,)), dma((Z,)),
    ]
    any_spec = pl.BlockSpec(memory_space=pl.ANY)
    vmem_spec = pl.BlockSpec(memory_space=pltpu.VMEM)
    smem_spec = pl.BlockSpec(memory_space=pltpu.SMEM)
    return pl.pallas_call(
        functools.partial(kernel, sections, Z, X, C),
        out_shape=jax.ShapeDtypeStruct((1, rows, width), f32),
        in_specs=[any_spec, any_spec, vmem_spec, any_spec, any_spec, smem_spec, vmem_spec],
        out_specs=vmem_spec,
        scratch_shapes=scratch,
        compiler_params=pltpu.CompilerParams(
            collective_id=0, has_side_effects=True, vmem_limit_bytes=62 * 2**20
        ),
        name="arcface_head",
    )(
        inputs.reshape(sections, rows, dim), section_weight[0], section_gain, neck_weight,
        flat, sampled, labels,
    )


def solution(mesh):
    Z, X, C = split_of(mesh.shape["ident"])
    in_specs = (
        P("ident", None, None),
        P("section", None, None),
        P("section", None),
        P(),
        P("ident", None, None, None, None),
        P("ident", None),
        P("ident", "section"),
    )
    out_specs = P("ident", "section", None)
    return jax.shard_map(
        functools.partial(shards, Z, X, C),
        mesh=mesh, in_specs=in_specs, out_specs=out_specs, check_vma=False,
    )
```

time: 220 us -> 51.7 us (0.24)
  waiting for transfers between devices: 112 us -> 0 us
  blocking collectives: 53.5 us -> 0 us
  Pallas kernels: 0 us -> 49.9 us
  other arithmetic: 18.5 us -> 0 us
  matrix products: 15.4 us -> 0 us
  between operations: 13.3 us -> 0.01 us
  starting transfers between devices: 4.98 us -> 0 us
    reduce_scatter x1 -> x0, waiting for transfers between devices: 63.6 us -> none  [shards(): lax.psum_scatter(jnp.dot(pulled, unit_centers, preferred_element_type=jnp...]
    pallas_call x0 -> x1, Pallas kernels: none -> 49.9 us  [shards(): pl.pallas_call(functools.partial(kernel, sections, Z, X, C), out_shape=ja...]
    psum x1 -> x0, blocking collectives: 32.3 us -> none  [shards(): totals = lax.psum(jnp.sum(exp_logits, axis=(1, 2)), 'ident')]
    psum x1 -> x0, waiting for transfers between devices: 24.6 us -> none  [broadcast(): return lax.psum(block, axis)]
    all_gather x1 -> x0, blocking collectives: 21.2 us -> none  [shards(): lax.all_gather(labels, 'ident', axis=0, tiled=True)]
    all_gather x1 -> x0, waiting for transfers between devices: 15.9 us -> none  [shards(): lax.all_gather(unit_own[None], 'ident', axis=0, tiled=True)]
    dot_general x5 -> x0, matrix products: 15.4 us -> none  [the longest x2 5.85 us: section_apply(): mixed = jnp.dot(normed, weight, preferred_element_type=jnp.float32)]
    ppermute x1 -> x0, waiting for transfers between devices: 8.32 us -> none  [from_behind(): return lax.ppermute(block, axis, route)]
  transfers between devices with their start and end apart: 4 -> 0, of which waited for: 4 -> 0; matrix products, arithmetic and copies ran while one was open for 1% -> 0% of each run, Pallas kernels for 0% -> 0%
where the time goes in v2:
time: 51.7 us; the launch traced here: 51.5 us
  Pallas kernels  49.9 us (97%)
  local copies, waits for them, and re-layouts  1.62 us (3%)
    pallas_call x1, Pallas kernels, shards(): pl.pallas_call(functools.partial(kernel, sections, Z, X, C), out_shape=ja...  49.9 us
    unnamed x1, local copies, waits for them, and re-layouts  1.62 us

profile of v2, /device:TPU:0, one launch (start us, length us, event | category | flops | bytes accessed | tf_op | source)
XLA Modules:
  0.0 51.5 jit_solution(642933566268034853)
XLA Ops:
  0.0 49.9 %arcface_head.1 = f32[1,96,512]{2,1,0:T(8,128)} custom-call(bf16[2,96,1024]{2,1,0:T(8,128)(2,1)} %bitcast.5, bf16[1024,1024]{1,0:T(8,128)(2,1)} %bitcast.3, f32[1,1024]{1,0:T(1,128)} %gain_ref.1, bf16[1024,512]{1,0:T(8,128)(2,1)} %neck_hbm.1, bf16[768,512]{1,0:T(8,128)(2,1)} %bitcast.4, s32[1,2]{1,0:T(1,128)} %sampled_ref.1, s32[1,96]{1,0:T(1,128)} %labels_ref.1), custom_call_target="tpu_custom_call" | custom-call | tf_op jit(solution)/shard_map/arcface_head/pallas_call | solution.py:445
  49.9 1.6 %copy.9 = f32[1,96,512]{2,1,0:T(8,128)} copy(f32[1,96,512]{2,1,0:T(8,128)} %arcface_head.1) | data formatting | bytes 393216

commit v3 on v2

--- a/solution.py
+++ b/solution.py
@@ -34,21 +34,25 @@
 
 
 def kernel(
-    sections, Z, X, C,
+    sections, H, X, W, C,
     trunk_hbm, weight_hbm, gain_ref, neck_hbm, centers_hbm, sampled_ref, labels_ref,
     out_ref,
     trunk, weight, neck, raw, unit, hid_out, emb_send, emb, feats, labs, idents,
-    expo, coef_a, coef_b, tparts, tsum, pulled, send_z, recv_z,
+    expo, coef_a, coef_b, tparts, tsum, pulled, send_w, recv_w, send_h, recv_h,
     local_sem, hid_send_sem, hid_recv_sem, emb_send_sem, emb_recv_sem,
     id_send_sem, id_recv_sem, lab_send_sem, lab_recv_sem, t_send_sem, t_recv_sem,
-    rx_send_sem, rc_send_sem, r_recv_sem, f_send_sem, f_recv_sem, g_send_sem, g_recv_sem,
+    rx_send_sem, rc_send_sem, r_recv_sem, fh_send_sem, fw_send_sem, f_recv_sem,
+    gw_send_sem, gw_recv_sem, gh_send_sem, gh_recv_sem,
 ):
     Q = X * C
+    Z = H * W
     s = lax.axis_index("section")
     me = lax.axis_index("ident")
     c = lax.rem(me, C)
-    x = lax.rem(me // C, X)
-    z = me // Q
+    w = lax.rem(me // C, W)
+    x = lax.rem(me // (C * W), X)
+    h = me // (C * W * X)
+    z = h * W + w
     mine = x * C + c
     rows, width = emb.shape
     lanes = feats.shape[1]
@@ -56,10 +60,10 @@
     per_slot = nsub * nblk
 
     def in_row(q):
-        return (s, z * Q + q)
+        return (s, ((h * X + q // C) * W + w) * C + lax.rem(q, C))
 
     def at_z(zz):
-        return (s, zz * Q + mine)
+        return (s, ((zz // W * X + x) * W + lax.rem(zz, W)) * C + c)
 
     def remote(src, dst, send_sem, recv_sem, device):
         return pltpu.make_async_remote_copy(
@@ -212,6 +216,8 @@
 
         @pl.when(s < sections - 1)
         def _():
+            if j:
+                hid_copy(j - 1).wait_send()
             hid_copy(j).start()
 
         @pl.when(s == sections - 1)
@@ -236,46 +242,30 @@
     inverse = lax.rsqrt(jnp.sum(valf * valf, axis=-1, keepdims=True) + 1e-06)
     feats[z, 0:rows, :] = (valf * inverse).astype(jnp.bfloat16)
 
-    def near(k):
-        high = (2 * z) // Z
-        low = z + high * (Z - 1 - 2 * z)
-        index = k + (k - low + Z) // Z
-        return index + high * (Z - 1 - 2 * index)
-
-    def f_copy(src, zz, index):
+    def f_copy(src, zz, send_sem):
         part = feats.at[src, pl.ds(0, rows)]
-        return remote(part, part, f_send_sem.at[index], f_recv_sem.at[src], at_z(zz))
-
-    for k in range(Z - 1):
-        f_copy(z, near(k), k).start()
-
-    for d in range(1, X):
-        xx = lax.rem(x + d, X)
-        for a in range(nsamp):
-            r_arrived(xx * C + c, a)
-            for e in range(1, C):
-                rc_forward(xx, e, a).start()
-    for d in range(1, X):
-        xx = lax.rem(x + d, X)
-        prepare(xx * C + c)
-    for d in range(1, X):
-        xx = lax.rem(x + d, X)
-        for e in range(1, C):
-            q = xx * C + lax.rem(c + e, C)
-            for a in range(nsamp):
-                r_arrived(q, a)
-            prepare(q)
-    for d in range(1, Q):
-        q = lax.rem(mine + d, Q)
-        id_copy(q, q, 0).wait_recv()
-    for k in range(Z - 1):
-        lab_copy(near(k), near(k), 0).wait_recv()
+        return remote(part, part, send_sem, f_recv_sem.at[src], at_z(zz))
+
+    def fh_copy(d):
+        return f_copy(z, lax.rem(h + d, H) * W + w, fh_send_sem.at[d])
+
+    def fw_copy(i, d):
+        hh = lax.rem(h + i, H)
+        return f_copy(hh * W + w, h * W + lax.rem(w + d, W), fw_send_sem.at[i, d])
+
+    def f_arrived(zz):
+        f_copy(zz, zz, fh_send_sem.at[0]).wait_recv()
+
+    for d in range(1, H):
+        fh_copy(d).start()
+    for d in range(1, W):
+        fw_copy(0, d).start()
 
     tile = 32
     row_index = lax.broadcasted_iota(jnp.int32, (tile, lanes), 0)
     cos_m, sin_m = math.cos(margin_angle), math.sin(margin_angle)
 
-    def scores(zz):
+    def scores(zz, base, first_part):
         lab = jnp.broadcast_to(labs[zz, 0:1, :], (tile, lanes)) - row_index
 
         def shard(q, total):
@@ -311,23 +301,67 @@
                         expo[zz, q, a, k, at, :] = exps[k].astype(expo.dtype)
             return total
 
-        total = lax.fori_loop(0, Q, shard, jnp.zeros((tile, lanes), jnp.float32))
-        tparts[z, zz] = jnp.sum(total, axis=0, keepdims=True)
-
-    scores(z)
-    for k in range(Z - 1):
-        f_copy(near(k), near(k), 0).wait_recv()
-        scores(near(k))
+        total = lax.fori_loop(
+            base, base + C, shard, jnp.zeros((tile, lanes), jnp.float32)
+        )
+        total = jnp.sum(total, axis=0, keepdims=True)
+        tparts[z, zz] = total if first_part else tparts[z, zz] + total
+
+    for d in range(1, Q):
+        q = lax.rem(mine + d, Q)
+        id_copy(q, q, 0).wait_recv()
+    for d in range(1, Z):
+        zz = lax.rem(z + d, Z)
+        lab_copy(zz, zz, 0).wait_recv()
+
+    chip = x * C
+    scores(z, chip, True)
+    for d in range(1, W):
+        zz = h * W + lax.rem(w + d, W)
+        f_arrived(zz)
+        scores(zz, chip, True)
+    for i in range(1, H):
+        zz = lax.rem(h + i, H) * W + w
+        f_arrived(zz)
+        for d in range(1, W):
+            fw_copy(i, d).start()
+        scores(zz, chip, True)
+
+    for d in range(1, X):
+        xx = lax.rem(x + d, X)
+        for a in range(nsamp):
+            r_arrived(xx * C + c, a)
+            for e in range(1, C):
+                rc_forward(xx, e, a).start()
+    for i in range(1, H):
+        for d in range(1, W):
+            zz = lax.rem(h + i, H) * W + lax.rem(w + d, W)
+            f_arrived(zz)
+            scores(zz, chip, True)
+    for d in range(1, X):
+        xx = lax.rem(x + d, X)
+        prepare(xx * C + c)
+        for e in range(1, C):
+            q = xx * C + lax.rem(c + e, C)
+            for a in range(nsamp):
+                r_arrived(q, a)
+            prepare(q)
+
+    @pl.loop(0, Z)
+    def _(zz):
+        for d in range(1, X):
+            scores(zz, lax.rem(x + d, X) * C, False)
 
     def t_copy(src, zz, index):
         return remote(
             tparts.at[src], tparts.at[src], t_send_sem.at[index], t_recv_sem.at[src], at_z(zz)
         )
 
-    for k in range(Z - 1):
-        t_copy(z, near(k), k).start()
-    for k in range(Z - 1):
-        t_copy(near(k), near(k), 0).wait_recv()
+    for d in range(1, Z):
+        t_copy(z, lax.rem(z + d, Z), d).start()
+    for d in range(1, Z):
+        zz = lax.rem(z + d, Z)
+        t_copy(zz, zz, 0).wait_recv()
 
     tsum[...] = 1.0 / jnp.sum(tparts[...], axis=0)
 
@@ -352,22 +386,43 @@
         )
         return grad[0:rows]
 
-    def g_copy(zz):
-        return remote(
-            send_z.at[zz], recv_z.at[z], g_send_sem.at[zz], g_recv_sem.at[z], at_z(zz)
-        )
-
-    for k in reversed(range(Z - 1)):
-        send_z[near(k)] = backward(near(k)).astype(jnp.bfloat16)
-        g_copy(near(k)).start()
-    own_grad = backward(z)
-
-    for k in range(Z - 1):
-        zz = near(k)
+    def gw_copy(hh, ww):
+        return remote(
+            send_w.at[hh * W + ww], recv_w.at[w, hh],
+            gw_send_sem.at[hh * W + ww], gw_recv_sem.at[w, hh], at_z(h * W + ww),
+        )
+
+    def gh_copy(hh):
+        return remote(
+            send_h.at[hh], recv_h.at[h], gh_send_sem.at[hh], gh_recv_sem.at[h], at_z(hh * W + w)
+        )
+
+    def summed_over_w(hh):
+        value = backward(hh * W + w)
+        for d in range(1, W):
+            ww = lax.rem(w + d, W)
+            remote(
+                send_w.at[0], recv_w.at[ww, hh],
+                gw_send_sem.at[0], gw_recv_sem.at[ww, hh], at_z(z),
+            ).wait_recv()
+            value = value + recv_w[ww, hh].astype(jnp.float32)
+        return value
+
+    far = [lax.rem(h + i, H) for i in range(1, H)]
+    for hh in far + [h]:
+        for d in range(1, W):
+            ww = lax.rem(w + d, W)
+            send_w[hh * W + ww] = backward(hh * W + ww).astype(jnp.bfloat16)
+            gw_copy(hh, ww).start()
+    for hh in far:
+        send_h[hh] = summed_over_w(hh).astype(jnp.bfloat16)
+        gh_copy(hh).start()
+    own_grad = summed_over_w(h)
+    for hh in far:
         remote(
-            send_z.at[zz], recv_z.at[zz], g_send_sem.at[zz], g_recv_sem.at[zz], at_z(zz)
+            send_h.at[0], recv_h.at[hh], gh_send_sem.at[0], gh_recv_sem.at[hh], at_z(z)
         ).wait_recv()
-        own_grad = own_grad + recv_z[zz].astype(jnp.float32)
+        own_grad = own_grad + recv_h[hh].astype(jnp.float32)
 
     valf = emb[...].astype(jnp.float32)
     inverse = lax.rsqrt(jnp.sum(valf * valf, axis=-1, keepdims=True) + 1e-06)
@@ -378,7 +433,8 @@
     for j in range(sections):
         @pl.when(s < sections - 1)
         def _():
-            hid_copy(j).wait_send()
+            if j == sections - 1:
+                hid_copy(j).wait_send()
 
         if j < sections - 1:
             @pl.when(s == sections - 1)
@@ -396,15 +452,20 @@
                 rc_forward(lax.rem(x + d, X), e, a).wait_send()
         for d in range(1, C):
             rc_own(d, a).wait_send()
-    for k in range(Z - 1):
-        f_copy(z, near(k), k).wait_send()
-        t_copy(z, near(k), k).wait_send()
-        g_copy(near(k)).wait_send()
-
-
-def shards(Z, X, C, inputs, section_weight, section_gain, neck_weight, centers, sampled, labels):
+    for d in range(1, Z):
+        t_copy(z, lax.rem(z + d, Z), d).wait_send()
+    for d in range(1, H):
+        fh_copy(d).wait_send()
+        gh_copy(lax.rem(h + d, H)).wait_send()
+    for i in range(H):
+        for d in range(1, W):
+            fw_copy(i, d).wait_send()
+            gw_copy(lax.rem(h + i, H), lax.rem(w + d, W)).wait_send()
+
+
+def shards(H, X, W, C, inputs, section_weight, section_gain, neck_weight, centers, sampled, labels):
     sections = lax.axis_size("section")
-    Q = X * C
+    Q, Z = X * C, H * W
     dim = inputs.shape[-1]
     rows = inputs.shape[1] // sections
     _, nsamp, nsub, nblk, width = centers.shape
@@ -433,17 +494,19 @@
         vmem((Z, 1, lanes), f32),
         vmem((Q, nsamp * nsub * nblk, lanes), bf16),
         vmem((Z, rows, width), bf16),
-        vmem((Z, rows, width), bf16),
+        vmem((W, H, rows, width), bf16),
+        vmem((H, rows, width), bf16),
+        vmem((H, rows, width), bf16),
         dma((4,)), dma((sections,)), dma((sections,)), dma((sections,)), dma,
         dma((Q,)), dma((Q,)), dma((Z,)), dma((Z,)), dma((Z,)), dma((Z,)),
-        dma((X, nsamp)), dma((X, C, nsamp)), dma((Q, nsamp)), dma((Z,)), dma((Z,)),
-        dma((Z,)), dma((Z,)),
+        dma((X, nsamp)), dma((X, C, nsamp)), dma((Q, nsamp)),
+        dma((H,)), dma((H, W)), dma((Z,)), dma((Z,)), dma((W, H)), dma((H,)), dma((H,)),
     ]
     any_spec = pl.BlockSpec(memory_space=pl.ANY)
     vmem_spec = pl.BlockSpec(memory_space=pltpu.VMEM)
     smem_spec = pl.BlockSpec(memory_space=pltpu.SMEM)
     return pl.pallas_call(
-        functools.partial(kernel, sections, Z, X, C),
+        functools.partial(kernel, sections, H, X, W, C),
         out_shape=jax.ShapeDtypeStruct((1, rows, width), f32),
         in_specs=[any_spec, any_spec, vmem_spec, any_spec, any_spec, smem_spec, vmem_spec],
         out_specs=vmem_spec,
@@ -459,7 +522,9 @@
 
 
 def solution(mesh):
-    Z, X, C = split_of(mesh.shape["ident"])
+    depth, W, C = split_of(mesh.shape["ident"])
+    X = 2 if depth % 2 == 0 else 1
+    H = depth // X
     in_specs = (
         P("ident", None, None),
         P("section", None, None),
@@ -471,6 +536,6 @@
     )
     out_specs = P("ident", "section", None)
     return jax.shard_map(
-        functools.partial(shards, Z, X, C),
+        functools.partial(shards, H, X, W, C),
         mesh=mesh, in_specs=in_specs, out_specs=out_specs, check_vma=False,
     )

time: 51.7 us -> 56.4 us (1.091)
  Pallas kernels: 49.9 us -> 54.6 us
    pallas_call x1, Pallas kernels: 49.9 us -> 54.6 us  [shards(): pl.pallas_call(functools.partial(kernel, sections, H, X, W, C), out_shape...]
where the time goes in v3:
time: 56.4 us; the launch traced here: 56.3 us
  Pallas kernels  54.6 us (97%)
  local copies, waits for them, and re-layouts  1.62 us (3%)
    pallas_call x1, Pallas kernels, shards(): pl.pallas_call(functools.partial(kernel, sections, H, X, W, C), out_shape...  54.6 us
    unnamed x1, local copies, waits for them, and re-layouts  1.62 us

profile of v3, /device:TPU:0, one launch (start us, length us, event | category | flops | bytes accessed | tf_op | source)
XLA Modules:
  0.0 56.3 jit_solution(16696501385694843438)
XLA Ops:
  0.0 54.6 %arcface_head.1 = f32[1,96,512]{2,1,0:T(8,128)} custom-call(bf16[2,96,1024]{2,1,0:T(8,128)(2,1)} %bitcast.5, bf16[1024,1024]{1,0:T(8,128)(2,1)} %bitcast.3, f32[1,1024]{1,0:T(1,128)} %gain_ref.1, bf16[1024,512]{1,0:T(8,128)(2,1)} %neck_hbm.1, bf16[768,512]{1,0:T(8,128)(2,1)} %bitcast.4, s32[1,2]{1,0:T(1,128)} %sampled_ref.1, s32[1,96]{1,0:T(1,128)} %labels_ref.1), custom_call_target="tpu_custom_call" | custom-call | tf_op jit(solution)/shard_map/arcface_head/pallas_call | solution.py:508
  54.6 1.6 %copy.9 = f32[1,96,512]{2,1,0:T(8,128)} copy(f32[1,96,512]{2,1,0:T(8,128)} %arcface_head.1) | data formatting | bytes 393216
